TPU v7x, 512 devices: a whole 4x4x16 slice. The times are simulated.
512 devices in a mesh: enc: 16 (over z), seq: 8 (over x, core), tp: 4 (over y).
Axes of the slice: x: 4, y: 4, z: 16, core: 2. Of those that a mesh axis runs over, the one named last changes fastest.
Arguments:
- frames: bfloat16 [49152, 1280], P(('enc', 'seq'), 'tp'), may hold values from -6 to 6
- proj_weight: bfloat16 [1280, 8192], P('enc', 'tp'), may hold values from -0.15625 to 0.15625
- text_emb: bfloat16 [40960, 8192], P(('enc', 'seq'), 'tp')
- norm_gain: float32 [8192], P('tp'), may hold values from 0.1 to 1.9
- cotangent: bfloat16 [40960, 8192], P(('enc', 'seq'), 'tp'), may hold values from -6 to 6
- counts: int32 [128, 16], P(('enc', 'seq')), may hold values from 6 to 18, as said below
- offsets: int32 [128], P(('enc', 'seq')), may hold values from 0 to 32, as said below
Outputs:
- mixed: bfloat16 [40960, 8192], P(('enc', 'seq'), 'tp')
- grad_frames: bfloat16 [49152, 1280], P(('enc', 'seq'), 'tp')
Inputs may be any that keep to these rules, and one draw needn't show every extreme that they name: Each row of counts sums to 192, so every pooled row is placed. In every draw some q has counts[r, q] = 18 for every r. offsets[b] plus the pooled rows that token block b receives never exceeds 320, and reaches it for some b.
All inputs are finite; a program needn't handle non-finite values.
Results may differ from a plain program's by a relative error of at most 0.0052.
Values may be sent and summed in bfloat16 or wider, within the bound.
A program may use at most 64 MiB of HBM per device.

v0:
```python
import jax
import jax.numpy as jnp
from jax import lax
from jax.sharding import PartitionSpec as P

D = 8192


def body(frames, proj_weight, text_emb, norm_gain, cotangent, counts, offsets):
    enc_count = lax.axis_size("enc")
    pooled_rows = frames.shape[0] // 2
    part_width = frames.shape[1]
    mean_share = pooled_rows // enc_count
    slot_count = mean_share + mean_share // 2
    token_rows = text_emb.shape[0]
    pooled = (
        jnp.sum(frames.reshape(pooled_rows, 2, part_width).astype(jnp.float32), axis=1) * 0.5
    ).astype(jnp.bfloat16)
    send_counts = counts[0]
    row_start = jnp.cumsum(send_counts) - send_counts
    slot_index = jnp.arange(slot_count, dtype=jnp.int32)
    source_row = (row_start[:, None] + slot_index[None, :]).reshape(-1)
    slot_live = (slot_index[None, :] < send_counts[:, None]).reshape(-1)
    packing = (
        (source_row[:, None] == jnp.arange(pooled_rows, dtype=jnp.int32)[None, :])
        & slot_live[:, None]
    ).astype(jnp.bfloat16)
    counts_sent = send_counts.reshape(enc_count, 1).astype(jnp.bfloat16)
    whole_feat = lax.all_gather(pooled, "tp", axis=1, tiled=True)
    projected = jnp.dot(
        whole_feat,
        lax.all_gather(proj_weight, "enc", axis=0, tiled=True),
        preferred_element_type=jnp.float32,
    ).astype(jnp.bfloat16)
    outgoing = jnp.dot(packing, projected, preferred_element_type=jnp.float32).astype(jnp.bfloat16)
    audio_buf, arrived = (
        lax.all_to_all(outgoing, "enc", split_axis=0, concat_axis=0, tiled=True),
        lax.all_to_all(counts_sent, "enc", split_axis=0, concat_axis=0, tiled=True),
    )
    recv_counts = arrived[:, 0].astype(jnp.int32)
    recv_start = jnp.cumsum(recv_counts) - recv_counts
    token_pos = (offsets[0] + recv_start[:, None] + slot_index[None, :]).reshape(-1)
    live_slot = (slot_index[None, :] < recv_counts[:, None]).reshape(-1)
    placing = (
        (jnp.arange(token_rows, dtype=jnp.int32)[:, None] == token_pos[None, :])
        & live_slot[None, :]
    ).astype(jnp.bfloat16)
    placed = jnp.dot(placing, audio_buf, preferred_element_type=jnp.float32)
    audio_here = jnp.sum(placing.astype(jnp.float32), axis=1, keepdims=True) > 0.5
    hidden = jnp.where(audio_here, placed, text_emb.astype(jnp.float32))
    squares = lax.psum(jnp.sum(hidden * hidden, axis=1), "tp")
    inv_rms = lax.rsqrt(squares / D + 1e-05)[:, None]
    mixed = (hidden * inv_rms * norm_gain).astype(jnp.bfloat16)
    weighted = cotangent.astype(jnp.float32) * norm_gain
    slope_term = (lax.psum(jnp.sum(weighted * hidden, axis=1), "tp") / D)[:, None]
    grad_hidden = (inv_rms * weighted - inv_rms**3 * hidden * slope_term).astype(jnp.bfloat16)
    grad_buf = lax.dot_general(
        placing, grad_hidden, (((0,), (0,)), ((), ())), preferred_element_type=jnp.float32
    ).astype(jnp.bfloat16)
    returned = lax.all_to_all(grad_buf, "enc", split_axis=0, concat_axis=0, tiled=True)
    grad_rows = lax.dot_general(
        packing, returned, (((0,), (0,)), ((), ())), preferred_element_type=jnp.float32
    ).astype(jnp.bfloat16)
    grad_pooled = lax.psum_scatter(
        lax.dot_general(
            grad_rows,
            lax.all_gather(proj_weight, "enc", axis=0, tiled=True),
            (((1,), (1,)), ((), ())),
            preferred_element_type=jnp.float32,
        ),
        "tp",
        scatter_dimension=1,
        tiled=True,
    ).astype(jnp.bfloat16)
    halved = (grad_pooled.astype(jnp.float32) * 0.5)[:, None, :]
    grad_frames = (
        jnp.broadcast_to(halved, (pooled_rows, 2, part_width))
        .reshape(2 * pooled_rows, part_width)
        .astype(jnp.bfloat16)
    )
    return (mixed, grad_frames)


def solution(mesh):
    in_specs = (
        P(("enc", "seq"), "tp"),
        P("enc", "tp"),
        P(("enc", "seq"), "tp"),
        P("tp"),
        P(("enc", "seq"), "tp"),
        P(("enc", "seq"), None),
        P(("enc", "seq")),
    )
    out_specs = (P(("enc", "seq"), "tp"), P(("enc", "seq"), "tp"))
    return jax.shard_map(body, mesh=mesh, in_specs=in_specs, out_specs=out_specs, check_vma=False)
```

profile of v0, /device:TPU:2, one launch (start us, length us, event | category | flops | bytes accessed | tf_op | source)
XLA Modules:
  0.0 315.4 jit_solution(6932950216540985838)
XLA Ops:
  8.6 0.7 copy.29
  9.3 15.2 %all-to-all-start = ((bf16[16,1,1]{2,1,0:T(2,128)(2,1)}), bf16[16,1,1]{2,1,0:T(2,128)(2,1)S(1)}, u32[]{:S(2)}, u32[]{:S(2)}) async-start(bf16[16,1,1]{2,1,0:T(2,128)(2,1)} %copy.29), calls=%async_computation | async-start | bytes 16384 | tf_op jit(solution)/shard_map/all_to_all | solution.py:38
  24.5 0.7 iota_compare_fusion.2
  25.3 0.7 copy.31
  27.0 1.1 copy.32
  28.5 0.7 reduce_sum.37
  29.2 13.4 %all-gather = bf16[4,320,192]{1,2,0:T(8,128)(2,1)S(1)} all-gather(bf16[1,320,192]{1,2,0:T(8,128)(2,1)S(1)} %fusion.16), channel_id=1, replica_groups=mesh['enc'=16,'seq'=8,'tp'=4] {'tp'}, dimensions={0}, use_global_device_ids=true | all-gather | bytes 614400 | tf_op jit(solution)/shard_map/all_gather | solution.py:29
  43.6 52.3 %all-gather.3.cloned.1.call-done = bf16[1280,2048]{1,0:T(8,128)(2,1)} async-done(((bf16[80,2048]{1,0:T(8,128)(2,1)}), bf16[1280,2048]{1,0:T(8,128)(2,1)}) %all-gather.3.cloned.1.call-update) | async-done | bytes 5242896 | tf_op jit(solution)/shard_map/all_gather | solution.py:32
  95.8 4.0 %convolution_convert_fusion = bf16[288,2048]{1,0:T(8,128)(2,1)S(1)} fusion(bf16[1280,192]{0,1:T(8,128)(2,1)S(1)} %reshape.173, bf16[1280,2048]{1,0:T(8,128)(2,1)} %all-gather.3.cloned.1.call-done, s32[288]{0:T(512)S(1)} %add.77, pred[288]{0:T(512)(128)(4,1)S(1)} %lt.41), kind=kOutput, calls=%fused_computation.2 | convolution fusion | flops 1234219008 | bytes 6915488 | tf_op jit(solution)/shard_map/dot_general | solution.py:35
  99.8 1.4 all_to_all.21
  101.2 7.0 %all-to-all-start.1 = ((bf16[16,18,2048]{2,1,0:T(8,128)(2,1)}), bf16[16,18,2048]{2,1,0:T(8,128)(2,1)S(1)}, u32[]{:S(2)}, u32[]{:S(2)}) async-start(bf16[16,18,2048]{2,1,0:T(8,128)(2,1)} %all_to_all.21), calls=%async_computation.1 | async-start | bytes 3145728 | tf_op jit(solution)/shard_map/all_to_all | solution.py:37
  110.0 63.0 %all-to-all-done.1 = bf16[16,18,2048]{2,1,0:T(8,128)(2,1)S(1)} async-done(((bf16[16,18,2048]{2,1,0:T(8,128)(2,1)}), bf16[16,18,2048]{2,1,0:T(8,128)(2,1)S(1)}, u32[]{:S(2)}, u32[]{:S(2)}) %all-to-all-start.1) | async-done | bytes 1179680 | tf_op jit(solution)/shard_map/all_to_all | solution.py:37
  173.0 1.2 all_to_all.23
  174.2 3.5 %multiply_reduce_fusion = (f32[320]{0:T(512)S(1)}, f32[320]{0:T(512)S(1)}, f32[320,2048]{1,0:T(8,128)S(1)}) fusion(bf16[320,2048]{1,0:T(8,128)(2,1)} %param.11, f32[2048]{0:T(1024)S(1)} %copy-done.2, bf16[320,2048]{1,0:T(8,128)(2,1)} %param.9, bf16[288,2048]{1,0:T(8,128)(2,1)} %all_to_all.23, s32[288]{0:T(512)S(1)} %add.72, pred[288]{0:T(512)(128)(4,1)S(1)} %lt.38, ...), kind=kOutput, calls=%fused_computation.5 | convolution fusion | flops 382913920 | bytes 6435040 | tf_op jit(solution)/shard_map/dot_general | solution.py:48
  177.8 10.7 %all-reduce = (f32[320]{0:T(512)S(1)}, f32[320]{0:T(512)S(1)}) all-reduce(f32[320]{0:T(512)S(1)} %get-tuple-element.11, f32[320]{0:T(512)S(1)} %get-tuple-element.10), channel_id=1, replica_groups=mesh['enc'=16,'seq'=8,'tp'=4] {'tp'}, use_global_device_ids=true, to_apply=%region_5.6 | all-reduce | flops 640 | bytes 5120 | tf_op jit(solution)/shard_map/psum | solution.py:51
  188.5 3.4 %convolution_convert_fusion.1 = bf16[288,2048]{1,0:T(8,128)(2,1)} fusion(f32[320,2048]{1,0:T(8,128)S(1)} %get-tuple-element.16, bf16[320,2048]{1,0:T(8,128)(2,1)} %param.11, f32[320]{0:T(512)S(1)} %get-tuple-element.17, f32[320]{0:T(512)S(1)} %get-tuple-element.14, f32[2048]{0:T(1024)S(1)} %copy-done.2, f32[320]{0:T(512)S(1)} %get-tuple-element.15, ...), kind=kOutput, calls=%fused_computation.3 | convolution fusion | flops 382849024 | bytes 5125280 | tf_op jit(solution)/shard_map/dot_general | solution.py:57
  191.8 1.4 all_to_all.24
  193.3 79.3 %all_to_all.30 = bf16[16,18,2048]{2,1,0:T(8,128)(2,1)S(1)} all-to-all(bf16[16,18,2048]{2,1,0:T(8,128)(2,1)S(1)} %all_to_all.24), channel_id=1, replica_groups=mesh['enc'=16,'seq'=8,'tp'=4] {'enc'}, dimensions={0} | all-to-all | bytes 2359296 | tf_op jit(solution)/shard_map/all_to_all | solution.py:60
  272.5 1.2 all_to_all.26
  273.7 6.3 %convolution_bitcast_fusion = f32[1280,192]{1,0:T(8,128)} fusion(bf16[1280,2048]{1,0:T(8,128)(2,1)} %all-gather.3.cloned.1.call-done, bf16[288,2048]{1,0:T(8,128)(2,1)} %all_to_all.26, s32[288]{0:T(512)S(1)} %add.77, pred[288]{0:T(512)(128)(4,1)S(1)} %lt.41), kind=kOutput, calls=%fused_computation.1 | convolution fusion | flops 1233629184 | bytes 7407008
  280.1 1.3 multiply_convert_fusion
  281.4 24.7 %reduce-scatter.4.cloned.1.call-done = f32[320,192]{1,0:T(8,128)} async-done(((f32[1280,192]{1,0:T(8,128)}), f32[320,192]{1,0:T(8,128)}) %reduce-scatter.4.cloned.1.call-update) | async-done | bytes 245776
  306.1 1.1 copy.36
  307.7 0.9 copy.34
  (37 shorter events, 5.3 us)
Async XLA Ops:
  7.2 88.7 %all-gather.3.cloned.1.call-start = ((), (), s32[]{:S(2)}) async-start(), calls=%async_computation.4 | async-start | bytes 5570560 | tf_op jit(solution)/shard_map/all_gather | solution.py:32
  9.3 92.0 %all-to-all-start = ((bf16[16,1,1]{2,1,0:T(2,128)(2,1)}), bf16[16,1,1]{2,1,0:T(2,128)(2,1)S(1)}, u32[]{:S(2)}, u32[]{:S(2)}) async-start(bf16[16,1,1]{2,1,0:T(2,128)(2,1)} %copy.29), calls=%async_computation | async-start | bytes 16384 | tf_op jit(solution)/shard_map/all_to_all | solution.py:38
  101.2 73.0 %copy-start.2 = (f32[2048]{0:T(1024)S(1)}, f32[2048]{0:T(1024)}, u32[]{:S(2)}) copy-start(f32[2048]{0:T(1024)} %param.10) | copy-start | bytes 24580
  101.2 71.8 %all-to-all-start.1 = ((bf16[16,18,2048]{2,1,0:T(8,128)(2,1)}), bf16[16,18,2048]{2,1,0:T(8,128)(2,1)S(1)}, u32[]{:S(2)}, u32[]{:S(2)}) async-start(bf16[16,18,2048]{2,1,0:T(8,128)(2,1)} %all_to_all.21), calls=%async_computation.1 | async-start | bytes 3145728 | tf_op jit(solution)/shard_map/all_to_all | solution.py:37
  108.2 197.8 %reduce-scatter.4.cloned.1.call-start = ((), (), s32[]{:S(2)}) async-start(), calls=%async_computation.5 | async-start | bytes 1638400
  177.8 10.7 %copy-start = (f32[320,2048]{1,0:T(8,128)}, f32[320,2048]{1,0:T(8,128)S(1)}, u32[]{:S(2)}) copy-start(f32[320,2048]{1,0:T(8,128)S(1)} %get-tuple-element.16) | copy-start | bytes 7864324
  273.7 6.3 %copy-start.1 = (f32[320,2048]{1,0:T(8,128)S(1)}, f32[320,2048]{1,0:T(8,128)}, u32[]{:S(2)}) copy-start(f32[320,2048]{1,0:T(8,128)} %copy-done) | copy-start | bytes 7864324
Sparse Core Ops, SparseCore 0:
  10.1 85.7 all-gather.2
  280.2 25.8 reduce-scatter.3
where the time goes:
time: 316 us; the launch traced here: 315 us
  waiting for transfers between devices  141 us (45%)
  blocking collectives  103 us (33%)
  starting transfers between devices  22.3 us (7%)
  matrix products  17.2 us (5%)
  between operations  14.8 us (5%)
  local copies, waits for them, and re-layouts  11.8 us (4%)
  other arithmetic  5.26 us (2%)
    all_to_all x1, blocking collectives, body(): lax.all_to_all(grad_buf, 'enc', split_axis=0, concat_axis=0, tiled=True)  79.3 us
    all_to_all x1, waiting for transfers between devices, body(): lax.all_to_all(outgoing, 'enc', split_axis=0, concat_axis=0, tiled=True)  63 us
    all_gather x1, waiting for transfers between devices, body(): lax.all_gather(proj_weight, 'enc', axis=0, tiled=True)  52.3 us
    unnamed x3, waiting for transfers between devices  25.4 us
    all_to_all x1, starting transfers between devices, body(): lax.all_to_all(counts_sent, 'enc', split_axis=0, concat_axis=0, tiled=True)  15.2 us
    all_gather x1, blocking collectives, body(): whole_feat = lax.all_gather(pooled, 'tp', axis=1, tiled=True)  13.4 us
    psum x1, blocking collectives, body(): squares = lax.psum(jnp.sum(hidden * hidden, axis=1), 'tp')  10.7 us
    all_to_all x1, starting transfers between devices, body(): lax.all_to_all(outgoing, 'enc', split_axis=0, concat_axis=0, tiled=True)  7 us
  transfers between devices with their start and end apart: 4, of which 3 were waited for; matrix products, arithmetic and copies ran while one was open for 4% of the time, Pallas kernels for 0%

commit v1 on v0

v1 whole, which is shorter than its diff:
```python
import jax
import jax.numpy as jnp
from jax import lax
from jax.experimental import pallas as pl
from jax.experimental.pallas import tpu as pltpu
from jax.sharding import PartitionSpec as P

D = 8192
EPS = 1e-05
MESH = pl.DeviceIdType.MESH
F32 = jnp.float32
BF16 = jnp.bfloat16

N_ENC = 16
N_X = 4
N_TP = 4
CHUNK = 80
WIDE = 2048
PART = 320
SLAB = 512
HALF = 256
SLOT = 16
SLOTS = N_ENC * SLOT
LANES = 384
TOKENS = 320
HOPS = 8
STREAMS = ((0, 0), (1, 1), (0, 1), (1, 0))


def nt(a, b):
    return lax.dot_general(a, b, (((1,), (1,)), ((), ())), preferred_element_type=F32)


def nn(a, b):
    return jnp.dot(a, b, preferred_element_type=F32)


def identity(size):
    rows = lax.broadcasted_iota(jnp.int32, (size, size), 0)
    cols = lax.broadcasted_iota(jnp.int32, (size, size), 1)
    return (rows == cols).astype(F32).astype(BF16)


def slot_maps(start, count, target, value):
    place = jnp.bitwise_and(lax.broadcasted_iota(jnp.int32, target.shape, 0), SLOT - 1)
    placef = place.astype(F32)
    main = (start + placef == target) & (placef < count)
    extra = jnp.where(place >= 5, 17.0, 16.0)
    spare = (start + extra == target) & (extra < count) & (place < 10)
    zero = jnp.zeros_like(target)
    return jnp.where(main, value, zero).astype(BF16), jnp.where(spare, value, zero).astype(BF16)


def piece_mask(shape, axis, piece):
    place = jnp.bitwise_and(lax.broadcasted_iota(jnp.int32, shape, axis), SLOT - 1)
    return (place == piece) | (place == piece + 5)


def encode(main, spare, items):
    low = nt(main, items[0:256])
    none = jnp.zeros((64, items.shape[1]), BF16)
    high = nt(main, jnp.concatenate([items[256:320], none], axis=0))
    for piece in range(5):
        part = nt(spare, jnp.concatenate([none, items[64 * piece : 64 * piece + 64]], axis=0))
        high = high + jnp.where(piece_mask(part.shape, 0, piece), part, 0.0)
    return low, high


def decode(slots, main, spare, eye):
    turned = nt(eye, slots)
    rest = turned[320:384]
    pieces = [jnp.where(piece_mask(rest.shape, 1, piece), rest, 0.0) for piece in range(5)]
    stacked = jnp.concatenate(pieces, axis=0).astype(BF16)
    return nn(turned[0:320].astype(BF16), main) + nn(stacked, spare)


def column(row, size):
    return jnp.transpose(jnp.broadcast_to(row, (128, size)))


def kernel(
    frames, weight, text, gain, cot, counts, offset, mixed, grads,
    wfull, textv, cotv, hid, gh, mixv, turned, pooled, slots, ygat, ysend, yrecv, stats, sums, bsend, bret, fmap, tmap,
    zs, zr, xs, xr, as_, ar, bs, br, fs, fr, ys, yr, ss, sr, rs, rr, gs, gr, ls,
):
    e, s, t = lax.axis_index("enc"), lax.axis_index("seq"), lax.axis_index("tp")
    core = lax.rem(s, 2)
    chip = lax.div(s, 2)
    other = s + 1 - 2 * core
    x_next = lax.rem(chip + 1, N_X) * 2 + core
    x_prev = lax.rem(chip + N_X - 1, N_X) * 2 + core
    side = lax.rem(chip, 2)
    my_col = pl.multiple_of((side * 2 + core) * SLAB, SLAB)
    x_col = pl.multiple_of(((1 - side) * 2 + core) * SLAB, SLAB)

    def enc_at(step):
        return lax.rem(e + step + 2 * N_ENC, N_ENC)

    def tp_at(step):
        return lax.rem(t + step, N_TP)

    barrier = pltpu.get_barrier_semaphore()

    def greet(step, carry):
        pl.semaphore_signal(barrier, inc=1, device_id={"enc": enc_at(step)}, device_id_type=MESH)
        return carry

    lax.fori_loop(1, N_ENC, greet, 0)
    for step in range(1, N_TP):
        pl.semaphore_signal(barrier, inc=1, device_id={"tp": tp_at(step)}, device_id_type=MESH)
    for peer in (other, x_next, x_prev):
        pl.semaphore_signal(barrier, inc=1, device_id={"seq": peer}, device_id_type=MESH)

    own_rows = pl.ds(pl.multiple_of(e * CHUNK, CHUNK), CHUNK)
    locals_in = [
        pltpu.make_async_copy(weight, wfull.at[own_rows, :], ls.at[0]),
        pltpu.make_async_copy(text, textv, ls.at[1]),
        pltpu.make_async_copy(cot, cotv, ls.at[2]),
    ]
    for copy in locals_in:
        copy.start()

    row = lax.broadcasted_iota(jnp.int32, (SLOTS, N_ENC), 0)
    lane = lax.broadcasted_iota(jnp.int32, (SLOTS, N_ENC), 1)
    dealt = jnp.broadcast_to(counts[...].astype(F32), (SLOTS, N_ENC))
    block = jnp.right_shift(row, 4)
    count = jnp.sum(jnp.where(lane == block, dealt, 0.0), axis=1, keepdims=True)
    start = jnp.sum(jnp.where(lane < block, dealt, 0.0), axis=1, keepdims=True)
    target = jnp.right_shift(lax.broadcasted_iota(jnp.int32, (SLOTS, LANES), 1), 1).astype(F32)
    main, spare = slot_maps(start, count, target, 0.5)
    fmap[0] = main
    fmap[1] = spare
    low, high = encode(main, spare, frames[...])
    place = jnp.bitwise_and(lax.broadcasted_iota(jnp.int32, high.shape, 0), SLOT - 1)
    in_spare = lax.broadcasted_iota(jnp.int32, high.shape, 1) >= 64
    high = jnp.where((place >= 10) & in_spare, count, high)
    slots[:, 0:256] = low.astype(BF16)
    slots[:, 256:384] = high.astype(BF16)

    pl.semaphore_wait(barrier, N_ENC - 1 + N_TP - 1 + 3)

    def chunk_at(direction, hop):
        step = -(hop + 1) if direction == 0 else hop + 1
        return pl.ds(pl.multiple_of(enc_at(step) * CHUNK, CHUNK), CHUNK)

    def sem_at(direction, half, hop):
        return (direction * 2 + half) * HOPS + hop

    def z_copy(direction, half, hop, src, dst):
        index = sem_at(direction, half, hop)
        to = enc_at(1) if direction == 0 else enc_at(-1)
        return pltpu.make_async_remote_copy(
            src_ref=src, dst_ref=dst, send_sem=zs.at[index], recv_sem=zr.at[index],
            device_id={"enc": to}, device_id_type=MESH,
        )

    def seq_copy(ref, send, recv, index, to):
        return pltpu.make_async_remote_copy(
            src_ref=ref, dst_ref=ref, send_sem=send.at[index], recv_sem=recv.at[index],
            device_id={"seq": to}, device_id_type=MESH,
        )

    def own_slab(half):
        return pl.ds(pl.multiple_of(my_col + half * HALF, HALF), HALF)

    def x_slab(half):
        return pl.ds(pl.multiple_of(x_col + half * HALF, HALF), HALF)

    def first_hop(direction, half):
        return z_copy(direction, half, 0, weight.at[:, own_slab(half)], wfull.at[own_rows, own_slab(half)])

    def next_hop(direction, half, hop):
        ref = wfull.at[chunk_at(direction, hop - 1), own_slab(half)]
        return z_copy(direction, half, hop, ref, ref)

    def landed(direction, half, hop):
        ref = wfull.at[chunk_at(direction, hop), own_slab(half)]
        return z_copy(direction, half, hop, ref, ref)

    def x_copy(direction, half, hop):
        ref = wfull.at[chunk_at(direction, hop), own_slab(half)]
        return seq_copy(ref, xs, xr, sem_at(direction, half, hop), x_next if half == 0 else x_prev)

    def x_landed(direction, half, hop):
        ref = wfull.at[chunk_at(direction, hop), x_slab(half)]
        return seq_copy(ref, xs, xr, sem_at(direction, half, hop), x_next if half == 0 else x_prev)

    def core_copy(direction, half, hop):
        ref = wfull.at[chunk_at(direction, hop), own_slab(half)]
        return seq_copy(ref, as_, ar, sem_at(direction, half, hop), other)

    def core_relay(direction, half, hop):
        ref = wfull.at[chunk_at(direction, hop), x_slab(half)]
        return seq_copy(ref, bs, br, sem_at(direction, half, hop), other)

    def slot_rows(index):
        return pl.ds(pl.multiple_of(index * SLOT, SLOT), SLOT)

    def pooled_copy(step):
        return pltpu.make_async_remote_copy(
            src_ref=slots.at[slot_rows(enc_at(step)), :], dst_ref=ygat.at[t, slot_rows(e), :],
            send_sem=fs.at[step], recv_sem=fr.at[step], device_id={"enc": enc_at(step)}, device_id_type=MESH,
        )

    def pooled_landed(step):
        ref = ygat.at[t, slot_rows(enc_at(-step)), :]
        return pltpu.make_async_remote_copy(
            src_ref=ref, dst_ref=ref, send_sem=fs.at[step], recv_sem=fr.at[step],
            device_id={"enc": enc_at(step)}, device_id_type=MESH,
        )

    def each(low_step, high_step, do):
        def body(step, carry):
            do(step)
            return carry

        lax.fori_loop(low_step, high_step, body, 0)

    for direction, half in STREAMS:
        first_hop(direction, half).start()
    each(1, N_ENC, lambda step: pooled_copy(step).start())
    ygat[t, slot_rows(e), :] = slots[slot_rows(e), :]

    def arrive(hop, streams, onward):
        for direction, half in streams:
            landed(direction, half, hop).wait_recv()
            if (direction, half) in onward:
                next_hop(direction, half, hop + 1).start()
            x_copy(direction, half, hop).start()
            core_copy(direction, half, hop).start()

    def relay(hop, streams):
        for direction, half in streams:
            x_landed(direction, half, hop).wait_recv()
            core_relay(direction, half, hop).start()

    arrive(0, STREAMS, STREAMS)

    def ring(hop):
        arrive(hop, STREAMS, STREAMS)
        relay(hop - 1, STREAMS)

    each(1, 3, ring)

    each(1, N_ENC, lambda step: pooled_landed(step).wait_recv())

    def part_copy(step):
        return pltpu.make_async_remote_copy(
            src_ref=ygat.at[t], dst_ref=ygat.at[t], send_sem=ys.at[step], recv_sem=yr.at[step],
            device_id={"tp": tp_at(step)}, device_id_type=MESH,
        )

    def part_landed(step):
        ref = ygat.at[tp_at(N_TP - step)]
        return pltpu.make_async_remote_copy(
            src_ref=ref, dst_ref=ref, send_sem=ys.at[step], recv_sem=yr.at[step],
            device_id={"tp": tp_at(step)}, device_id_type=MESH,
        )

    for step in (2, 1, 3):
        part_copy(step).start()
    each(3, HOPS - 2, ring)
    arrive(HOPS - 2, STREAMS, STREAMS[:2])
    relay(HOPS - 3, STREAMS)

    slot = lax.broadcasted_iota(jnp.int32, (SLOTS, SLOTS), 0)
    source = lax.broadcasted_iota(jnp.int32, (SLOTS, SLOTS), 1)
    last = jnp.bitwise_and(source, SLOT - 1) == SLOT - 1
    slot_of, source_of = jnp.right_shift(slot, 4), jnp.right_shift(source, 4)
    same = jnp.where((slot_of == source_of) & last, 1.0, 0.0).astype(BF16)
    before = jnp.where((source_of < slot_of) & last, 1.0, 0.0).astype(BF16)
    marks = ygat[t, :, 256:384]
    end_lane = lax.broadcasted_iota(jnp.int32, (SLOTS, 128), 1) == 127
    count = jnp.sum(jnp.where(end_lane, nn(same, marks), 0.0), axis=1, keepdims=True)
    start = jnp.sum(jnp.where(end_lane, nn(before, marks), 0.0), axis=1, keepdims=True)
    first = offset[0].astype(F32)
    end = jnp.max(start + count, axis=0, keepdims=True) + first
    target = lax.broadcasted_iota(jnp.int32, (SLOTS, LANES), 1).astype(F32) - first
    main, spare = slot_maps(start, count, target, 1.0)
    tmap[0] = main
    tmap[1] = spare

    for step in range(1, N_TP):
        part_landed(step).wait_recv()
    eye = identity(LANES)
    for part in range(N_TP):
        turned[PART * part : PART * part + PART, :] = decode(ygat[part], main, spare, eye).astype(BF16)
    pooled[...] = nt(eye, turned[...]).astype(BF16)

    arrive(HOPS - 1, STREAMS[:2], ())
    relay(HOPS - 2, STREAMS)
    relay(HOPS - 1, STREAMS[:2])

    def seq_waits(hop, streams):
        for direction, half in streams:
            core_copy_in = wfull.at[chunk_at(direction, hop), own_slab(half)]
            seq_copy(core_copy_in, as_, ar, sem_at(direction, half, hop), other).wait_recv()
            seq_copy(core_copy_in, bs, br, sem_at(direction, half, hop), other).wait_recv()

    each(0, HOPS - 1, lambda hop: seq_waits(hop, STREAMS))
    seq_waits(HOPS - 1, STREAMS[:2])
    for copy in locals_in:
        copy.wait()

    sums[...] = jnp.zeros_like(sums)

    def forward(index):
        cols = pl.ds(pl.multiple_of(index * HALF, HALF), HALF)
        projected = nn(pooled[0:TOKENS, :], wfull[:, cols]).astype(BF16).astype(F32)
        token = lax.broadcasted_iota(jnp.int32, projected.shape, 0).astype(F32)
        hidden = jnp.where((token >= first) & (token < end), projected, textv[:, cols].astype(F32))
        hid[:, cols] = hidden.astype(BF16)
        squares = hidden * hidden
        slopes = cotv[:, cols].astype(F32) * gain[:, cols] * hidden
        sums[0, 0:TOKENS, :] += squares[:, 0:128] + squares[:, 128:256]
        sums[1, 0:TOKENS, :] += slopes[:, 0:128] + slopes[:, 128:256]

    each(0, WIDE // HALF, forward)

    stats[0] = jnp.zeros((8, LANES), F32)
    stats[0, 0:1, :] = jnp.sum(jnp.transpose(sums[0]), axis=0, keepdims=True)
    stats[0, 1:2, :] = jnp.sum(jnp.transpose(sums[1]), axis=0, keepdims=True)

    def stat_copy(step):
        return pltpu.make_async_remote_copy(
            src_ref=stats.at[0], dst_ref=stats.at[step], send_sem=ss.at[step], recv_sem=sr.at[step],
            device_id={"tp": tp_at(step)}, device_id_type=MESH,
        )

    for step in (2, 1, 3):
        stat_copy(step).start()
    gh[TOKENS:LANES, :] = jnp.zeros((LANES - TOKENS, WIDE), BF16)
    for step in (2, 1, 3):
        stat_copy(step).wait_recv()
    total = (stats[0] + stats[1]) + (stats[2] + stats[3])
    inv_row = lax.rsqrt(total[0:1] / D + EPS)
    slope_row = total[1:2] / D
    inv = column(inv_row, LANES)[0:TOKENS, 0:1]
    back = column(inv_row * inv_row * inv_row * slope_row, LANES)[0:TOKENS, 0:1]

    def backward(index):
        cols = pl.ds(pl.multiple_of(index * HALF, HALF), HALF)
        hidden = hid[:, cols].astype(F32)
        gains = gain[:, cols]
        weighted = cotv[:, cols].astype(F32) * gains
        gh[0:TOKENS, cols] = (inv * weighted - back * hidden).astype(BF16)
        mixv[:, cols] = (hidden * inv * gains).astype(BF16)

    each(0, WIDE // HALF, backward)
    mixed_out = pltpu.make_async_copy(mixv, mixed, ls.at[3])
    mixed_out.start()

    def sum_copy(step):
        return pltpu.make_async_remote_copy(
            src_ref=ysend.at[step], dst_ref=yrecv.at[step], send_sem=rs.at[step], recv_sem=rr.at[step],
            device_id={"tp": tp_at(step)}, device_id_type=MESH,
        )

    main, spare = tmap[0], tmap[1]
    for step in (2, 1, 3, 0):
        rows = pl.ds(pl.multiple_of(tp_at(step) * PART, PART), PART)
        partial = nt(wfull[rows, :], gh[...]).astype(BF16)
        low, high = encode(main, spare, partial)
        ysend[step, :, 0:256] = low.astype(BF16)
        ysend[step, :, 256:384] = high.astype(BF16)
        if step:
            sum_copy(step).start()
    for step in (2, 1, 3):
        sum_copy(step).wait_recv()
    bsend[...] = (
        (ysend[0].astype(F32) + yrecv[1].astype(F32)) + (yrecv[2].astype(F32) + yrecv[3].astype(F32))
    ).astype(BF16)

    def back_copy(step):
        return pltpu.make_async_remote_copy(
            src_ref=bsend.at[slot_rows(enc_at(step)), :], dst_ref=bret.at[slot_rows(e), :],
            send_sem=gs.at[step], recv_sem=gr.at[step], device_id={"enc": enc_at(step)}, device_id_type=MESH,
        )

    def back_landed(step):
        ref = bret.at[slot_rows(enc_at(-step)), :]
        return pltpu.make_async_remote_copy(
            src_ref=ref, dst_ref=ref, send_sem=gs.at[step], recv_sem=gr.at[step],
            device_id={"enc": enc_at(step)}, device_id_type=MESH,
        )

    each(1, N_ENC, lambda step: back_copy(step).start())
    bret[slot_rows(e), :] = bsend[slot_rows(e), :]

    def sent(hop, streams):
        for direction, half in streams:
            landed(direction, half, hop).wait_send()
            x_copy(direction, half, hop).wait_send()
            core_copy(direction, half, hop).wait_send()
            core_relay(direction, half, hop).wait_send()

    each(0, HOPS - 1, lambda hop: sent(hop, STREAMS))
    sent(HOPS - 1, STREAMS[:2])
    each(1, N_ENC, lambda step: pooled_copy(step).wait_send())
    for step in range(1, N_TP):
        part_copy(step).wait_send()
        stat_copy(step).wait_send()
        sum_copy(step).wait_send()

    each(1, N_ENC, lambda step: back_landed(step).wait_recv())
    grads[...] = decode(bret[...], fmap[0], fmap[1], identity(LANES)).astype(BF16)
    each(1, N_ENC, lambda step: back_copy(step).wait_send())
    mixed_out.wait()


def body(frames, proj_weight, text_emb, norm_gain, cotangent, counts, offsets):
    any_space = pl.BlockSpec(memory_space=pl.ANY)
    vmem = pl.BlockSpec(memory_space=pltpu.VMEM)
    smem = pl.BlockSpec(memory_space=pltpu.SMEM)
    dma = pltpu.SemaphoreType.DMA
    mixed, grads = pl.pallas_call(
        kernel,
        out_shape=(
            jax.ShapeDtypeStruct((TOKENS, WIDE), BF16),
            jax.ShapeDtypeStruct((PART, LANES), BF16),
        ),
        in_specs=[vmem, any_space, any_space, vmem, any_space, vmem, smem],
        out_specs=(any_space, vmem),
        scratch_shapes=[
            pltpu.VMEM((N_ENC * CHUNK, WIDE), BF16),
            pltpu.VMEM((TOKENS, WIDE), BF16),
            pltpu.VMEM((TOKENS, WIDE), BF16),
            pltpu.VMEM((TOKENS, WIDE), BF16),
            pltpu.VMEM((LANES, WIDE), BF16),
            pltpu.VMEM((TOKENS, WIDE), BF16),
            pltpu.VMEM((N_ENC * CHUNK, LANES), BF16),
            pltpu.VMEM((LANES, N_ENC * CHUNK), BF16),
            pltpu.VMEM((SLOTS, LANES), BF16),
            pltpu.VMEM((N_TP, SLOTS, LANES), BF16),
            pltpu.VMEM((N_TP, SLOTS, LANES), BF16),
            pltpu.VMEM((N_TP, SLOTS, LANES), BF16),
            pltpu.VMEM((N_TP, 8, LANES), F32),
            pltpu.VMEM((2, LANES, 128), F32),
            pltpu.VMEM((SLOTS, LANES), BF16),
            pltpu.VMEM((SLOTS, LANES), BF16),
            pltpu.VMEM((2, SLOTS, LANES), BF16),
            pltpu.VMEM((2, SLOTS, LANES), BF16),
            *[dma((4 * HOPS,)) for _ in range(8)],
            *[dma((N_ENC,)) for _ in range(2)],
            *[dma((N_TP,)) for _ in range(6)],
            *[dma((N_ENC,)) for _ in range(2)],
            dma((4,)),
        ],
        compiler_params=pltpu.CompilerParams(
            collective_id=0, has_side_effects=True, vmem_limit_bytes=56 * 1024 * 1024
        ),
    )(frames.T, proj_weight, text_emb, norm_gain.reshape(1, WIDE), cotangent, counts, offsets)
    return mixed, grads.T


def solution(mesh):
    in_specs = (
        P(("enc", "seq"), "tp"),
        P("enc", "tp"),
        P(("enc", "seq"), "tp"),
        P("tp"),
        P(("enc", "seq"), "tp"),
        P(("enc", "seq"), None),
        P(("enc", "seq")),
    )
    out_specs = (P(("enc", "seq"), "tp"), P(("enc", "seq"), "tp"))
    return jax.shard_map(body, mesh=mesh, in_specs=in_specs, out_specs=out_specs, check_vma=False)
```

time: 316 us -> 97.5 us (0.31)
  the two profiles are of different devices: /device:TPU:2 before, /device:TPU:32 now
where the time goes in v1:
time: 97.5 us; the launch traced here: 97.4 us
  Pallas kernels  92.8 us (95%)
  local copies, waits for them, and re-layouts  3.26 us (3%)
  between operations  1.3 us (1%)
    pallas_call x1, Pallas kernels, body(): pl.pallas_call(kernel, out_shape=(jax.ShapeDtypeStruct((TOKENS, WIDE), BF...  92.8 us
    unnamed x4, local copies, waits for them, and re-layouts  3.26 us

profile of v1, /device:TPU:32, one launch (start us, length us, event | category | flops | bytes accessed | tf_op | source)
XLA Modules:
  0.0 97.4 jit_solution(3160755636048357003)
XLA Ops:
  1.3 92.8 %shard_map.86 = (bf16[320,2048]{1,0:T(8,128)(2,1)}, bf16[320,384]{1,0:T(8,128)(2,1)}) custom-call(bf16[320,384]{1,0:T(8,128)(2,1)} %bitcast.3, bf16[80,2048]{1,0:T(8,128)(2,1)} %weight.1, bf16[320,2048]{1,0:T(8,128)(2,1)} %text.1, f32[1,2048]{1,0:T(1,128)} %bitcast.5, bf16[320,2048]{1,0:T(8,128)(2,1)} %cot.1, s32[1,16]{1,0:T(1,128)} %counts.1, s32[1]{0:T(128)S(6)} %copy.11.offset), custom_call_target="tpu_custom_call" | custom-call | tf_op jit(solution)/shard_map/pallas_call | solution.py:416
  94.1 0.0 copy-start
  94.1 2.6 %copy.12 = bf16[320,2048]{1,0:T(8,128)(2,1)} copy(bf16[320,2048]{1,0:T(8,128)(2,1)} %get-tuple-element.8) | data formatting | bytes 2621440
  96.7 0.0 copy-done
  96.7 0.7 copy.13
Async XLA Ops:
  94.1 2.6 %copy-start = (bf16[320,384]{1,0:T(8,128)(2,1)S(1)}, bf16[320,384]{1,0:T(8,128)(2,1)}, u32[]{:S(2)}) copy-start(bf16[320,384]{1,0:T(8,128)(2,1)} %get-tuple-element.5) | copy-start | bytes 737284

commit v2 on v1

v2 whole, which is shorter than its diff:
```python
import jax
import jax.numpy as jnp
from jax import lax
from jax.experimental import pallas as pl
from jax.experimental.pallas import tpu as pltpu
from jax.sharding import PartitionSpec as P

D = 8192
EPS = 1e-05
MESH = pl.DeviceIdType.MESH
F32 = jnp.float32
BF16 = jnp.bfloat16

N_ENC = 16
N_X = 4
N_TP = 4
CHUNK = 80
WIDE = 2048
PART = 320
SLAB = 256
HALF = 128
SLOT = 16
SLOTS = N_ENC * SLOT
LANES = 384
TOKENS = 320
STAGES = 4
CLASSES = 4
GROUP = SLOTS // CLASSES


def nt(a, b):
    return lax.dot_general(a, b, (((1,), (1,)), ((), ())), preferred_element_type=F32)


def nn(a, b):
    return jnp.dot(a, b, preferred_element_type=F32)


def identity(size):
    rows = lax.broadcasted_iota(jnp.int32, (size, size), 0)
    cols = lax.broadcasted_iota(jnp.int32, (size, size), 1)
    return (rows == cols).astype(F32).astype(BF16)


def slot_maps(start, count, target, value):
    place = jnp.bitwise_and(lax.broadcasted_iota(jnp.int32, target.shape, 0), SLOT - 1)
    placef = place.astype(F32)
    main = (start + placef == target) & (placef < count)
    extra = jnp.where(place >= 5, 17.0, 16.0)
    spare = (start + extra == target) & (extra < count) & (place < 10)
    zero = jnp.zeros_like(target)
    return jnp.where(main, value, zero).astype(BF16), jnp.where(spare, value, zero).astype(BF16)


def piece_mask(shape, axis, piece):
    place = jnp.bitwise_and(lax.broadcasted_iota(jnp.int32, shape, axis), SLOT - 1)
    return (place == piece) | (place == piece + 5)


def distance(place):
    return jnp.bitwise_and(place, 3) * 4 + jnp.right_shift(place, 2)


def encode(main, spare, items):
    low = nt(main, items[0:256])
    none = jnp.zeros((64, items.shape[1]), BF16)
    high = nt(main, jnp.concatenate([items[256:320], none], axis=0))
    for piece in range(5):
        part = nt(spare, jnp.concatenate([none, items[64 * piece : 64 * piece + 64]], axis=0))
        high = high + jnp.where(piece_mask(part.shape, 0, piece), part, 0.0)
    return low, high


def decode(slots, main, spare, eye):
    turned = nt(eye, slots)
    rest = turned[320:384]
    pieces = [jnp.where(piece_mask(rest.shape, 1, piece), rest, 0.0) for piece in range(5)]
    stacked = jnp.concatenate(pieces, axis=0).astype(BF16)
    return nn(turned[0:320].astype(BF16), main) + nn(stacked, spare)


def column(row, size):
    return jnp.transpose(jnp.broadcast_to(row, (128, size)))


def kernel(
    frames_in, weight, text, gain_in, cot, counts_in, offset, mixed, grads,
    frames, gain, counts, wfull, textv, cotv, hid, gh, mixv, turned, pooled, slots, ygat, ysend, yrecv, stats, sums, bsend, bret, fmap, tmap,
    zs, zr, xs, xr, us, ur, cs, cr, fs, fr, ys, yr, ss, sr, rs, rr, gs, gr, ls,
):
    e, s, t = lax.axis_index("enc"), lax.axis_index("seq"), lax.axis_index("tp")
    core = lax.rem(s, 2)
    chip = lax.div(s, 2)
    other = s + 1 - 2 * core
    x_next = lax.rem(chip + 1, N_X) * 2 + core
    x_prev = lax.rem(chip + N_X - 1, N_X) * 2 + core

    def slab_at(step, which):
        return pl.multiple_of((lax.rem(chip + step, N_X) * 2 + which) * SLAB, SLAB)

    def enc_at(step):
        return lax.rem(e + step + 2 * N_ENC, N_ENC)

    def tp_at(step):
        return lax.rem(t + step, N_TP)

    barrier = pltpu.get_barrier_semaphore()

    def greet(step, carry):
        pl.semaphore_signal(barrier, inc=1, device_id={"enc": enc_at(step)}, device_id_type=MESH)
        return carry

    lax.fori_loop(1, N_ENC, greet, 0)
    for step in range(1, N_TP):
        pl.semaphore_signal(barrier, inc=1, device_id={"tp": tp_at(step)}, device_id_type=MESH)
    for peer in (other, x_next, x_prev):
        pl.semaphore_signal(barrier, inc=1, device_id={"seq": peer}, device_id_type=MESH)

    locals_in = [
        pltpu.make_async_copy(weight, wfull.at[0:CHUNK, :], ls.at[0]),
        pltpu.make_async_copy(text, textv, ls.at[1]),
        pltpu.make_async_copy(cot, cotv, ls.at[2]),
        pltpu.make_async_copy(gain_in, gain, ls.at[6]),
    ]
    first_in = [
        pltpu.make_async_copy(counts_in, counts, ls.at[4]),
        pltpu.make_async_copy(frames_in, frames, ls.at[5]),
    ]
    for copy in first_in:
        copy.start()

    pl.semaphore_wait(barrier, N_ENC - 1 + N_TP - 1 + 3)

    def chunk_rows(direction, far):
        return pl.ds(((N_ENC - far) if direction == 0 else far) * CHUNK, CHUNK)

    my_cols = pl.ds(slab_at(0, core), SLAB)

    def z_copy(direction, base, step):
        src = wfull.at[chunk_rows(direction, base), my_cols] if base else weight.at[:, my_cols]
        index = direction * 8 + base + step - 1
        return pltpu.make_async_remote_copy(
            src_ref=src, dst_ref=wfull.at[chunk_rows(direction, base + step), my_cols],
            send_sem=zs.at[index], recv_sem=zr.at[index],
            device_id={"enc": enc_at(step if direction == 0 else -step)}, device_id_type=MESH,
        )

    def reaches(direction, far):
        return far <= (8 if direction == 0 else 7)

    def z_sends(direction, base):
        for step in (2, 1):
            if reaches(direction, base + step):
                z_copy(direction, base, step).start()

    def z_landed(direction, far):
        step = 2 if far % 2 == 0 else 1
        z_copy(direction, far - step, step).wait_recv()

    def group_rows(direction, stage):
        if direction == 0:
            return pl.ds((N_ENC - 2 - 2 * stage) * CHUNK, 2 * CHUNK)
        return pl.ds((2 * stage + 1) * CHUNK, (2 if stage < STAGES - 1 else 1) * CHUNK)

    def seq_copy(ref, send, recv, index, to):
        return pltpu.make_async_remote_copy(
            src_ref=ref, dst_ref=ref, send_sem=send.at[index], recv_sem=recv.at[index],
            device_id={"seq": to}, device_id_type=MESH,
        )

    def x_copy(way, direction, stage):
        index = (way * 2 + direction) * STAGES + stage
        ref = wfull.at[group_rows(direction, stage), my_cols]
        return seq_copy(ref, xs, xr, index, x_next if way == 0 else x_prev)

    def x_landed(way, direction, stage):
        index = (way * 2 + direction) * STAGES + stage
        ref = wfull.at[group_rows(direction, stage), pl.ds(slab_at(3 if way == 0 else 1, core), SLAB)]
        seq_copy(ref, xs, xr, index, x_next if way == 0 else x_prev).wait_recv()

    def x_onward(way, direction, stage):
        index = (way * 2 + direction) * STAGES + stage
        cols = pl.ds(pl.multiple_of(slab_at(3 if way == 0 else 1, core) + way * HALF, HALF), HALF)
        return seq_copy(wfull.at[group_rows(direction, stage), cols], us, ur, index, x_next if way == 0 else x_prev)

    def far_landed(way, direction, stage):
        index = (way * 2 + direction) * STAGES + stage
        cols = pl.ds(pl.multiple_of(slab_at(2, core) + way * HALF, HALF), HALF)
        ref = wfull.at[group_rows(direction, stage), cols]
        seq_copy(ref, us, ur, index, x_next if way == 0 else x_prev).wait_recv()

    def core_copy(step, direction, stage, which):
        index = (step * 2 + direction) * STAGES + stage
        ref = wfull.at[group_rows(direction, stage), pl.ds(slab_at(step, which), SLAB)]
        return seq_copy(ref, cs, cr, index, other)

    def slot_rows(place):
        return pl.ds(pl.multiple_of(place * SLOT, SLOT), SLOT)

    def place_of(step):
        return lax.rem(step, 4) * 4 + lax.div(step, 4)

    def class_steps(kind):
        return (1 if kind == 0 else 0, 4), lambda index: 4 * index + kind

    def pooled_copy(step):
        return pltpu.make_async_remote_copy(
            src_ref=slots.at[slot_rows(place_of(step)), :],
            dst_ref=ygat.at[t, slot_rows(place_of(N_ENC - step)), :],
            send_sem=fs.at[step], recv_sem=fr.at[step], device_id={"enc": enc_at(step)}, device_id_type=MESH,
        )

    def pooled_landed(step):
        ref = ygat.at[t, slot_rows(place_of(N_ENC - step)), :]
        return pltpu.make_async_remote_copy(
            src_ref=ref, dst_ref=ref, send_sem=fs.at[step], recv_sem=fr.at[step],
            device_id={"enc": enc_at(step)}, device_id_type=MESH,
        )

    def each(low_step, high_step, do):
        def body(step, carry):
            do(step)
            return carry

        lax.fori_loop(low_step, high_step, body, 0)

    def each_of(kind, do):
        (low_index, high_index), step_of = class_steps(kind)
        each(low_index, high_index, lambda index: do(step_of(index)))

    for direction in (0, 1):
        z_sends(direction, 0)

    for copy in first_in:
        copy.wait()
    row = lax.broadcasted_iota(jnp.int32, (SLOTS, N_ENC), 0)
    lane = lax.broadcasted_iota(jnp.int32, (SLOTS, N_ENC), 1)
    dealt = jnp.broadcast_to(counts[...].astype(F32), (SLOTS, N_ENC))
    block = jnp.bitwise_and(distance(jnp.right_shift(row, 4)) + e, N_ENC - 1)
    count = jnp.sum(jnp.where(lane == block, dealt, 0.0), axis=1, keepdims=True)
    start = jnp.sum(jnp.where(lane < block, dealt, 0.0), axis=1, keepdims=True)
    target = jnp.right_shift(lax.broadcasted_iota(jnp.int32, (SLOTS, LANES), 1), 1).astype(F32)
    main, spare = slot_maps(start, count, target, 0.5)
    fmap[0] = main
    fmap[1] = spare
    low, high = encode(main, spare, frames[...])
    place = jnp.bitwise_and(lax.broadcasted_iota(jnp.int32, high.shape, 0), SLOT - 1)
    in_spare = lax.broadcasted_iota(jnp.int32, high.shape, 1) >= 64
    high = jnp.where((place >= 10) & in_spare, count, high)
    slots[:, 0:256] = low.astype(BF16)
    slots[:, 256:384] = high.astype(BF16)
    ygat[t, 0:SLOT, :] = slots[0:SLOT, :]

    def z_relay(stage):
        for direction in (0, 1):
            if reaches(direction, 2 * stage + 2):
                z_landed(direction, 2 * stage + 2)
                z_sends(direction, 2 * stage + 2)

    def seq_sends(stage):
        for direction in (0, 1):
            z_landed(direction, 2 * stage + 1)
            for way in (0, 1):
                x_copy(way, direction, stage).start()
            core_copy(0, direction, stage, core).start()

    def pooled_sends(kind):
        each_of(kind, lambda step: pooled_copy(step).start())

    def x_relay(stage):
        for direction in (0, 1):
            for way in (0, 1):
                x_landed(way, direction, stage)
                x_onward(way, direction, stage).start()
                core_copy(3 if way == 0 else 1, direction, stage, core).start()

    def far_relay(stage):
        for direction in (0, 1):
            for way in (0, 1):
                far_landed(way, direction, stage)
            core_copy(2, direction, stage, core).start()

    def from_core(step):
        for direction in (0, 1):
            for stage in range(STAGES):
                core_copy(step, direction, stage, 1 - core).wait_recv()

    def part_sem(step, kind):
        return step * CLASSES + kind

    def part_copy(step, kind):
        ref = ygat.at[t, pl.ds(kind * GROUP, GROUP), :]
        return pltpu.make_async_remote_copy(
            src_ref=ref, dst_ref=ref, send_sem=ys.at[part_sem(step, kind)], recv_sem=yr.at[part_sem(step, kind)],
            device_id={"tp": tp_at(step)}, device_id_type=MESH,
        )

    def part_landed(step, kind):
        ref = ygat.at[tp_at(N_TP - step), pl.ds(kind * GROUP, GROUP), :]
        return pltpu.make_async_remote_copy(
            src_ref=ref, dst_ref=ref, send_sem=ys.at[part_sem(step, kind)], recv_sem=yr.at[part_sem(step, kind)],
            device_id={"tp": tp_at(step)}, device_id_type=MESH,
        )

    def pass_on(kind):
        each_of((4 - kind) % 4, lambda step: pooled_landed(step).wait_recv())
        for step in (2, 1, 3):
            part_copy(step, kind).start()

    z_relay(0)
    pooled_sends(0)
    seq_sends(0)
    z_relay(1)
    pooled_sends(3)
    seq_sends(1)
    locals_in[0].start()
    locals_in[1].start()
    z_relay(2)
    pooled_sends(2)
    pooled_sends(1)
    seq_sends(2)
    locals_in[2].start()
    locals_in[3].start()
    x_relay(0)
    pass_on(0)
    z_relay(3)
    seq_sends(3)
    x_relay(1)
    pass_on(1)
    x_relay(2)
    pass_on(2)
    far_relay(0)
    x_relay(3)
    pass_on(3)
    far_relay(1)

    slot = lax.broadcasted_iota(jnp.int32, (SLOTS, SLOTS), 0)
    source = lax.broadcasted_iota(jnp.int32, (SLOTS, SLOTS), 1)
    last = jnp.bitwise_and(source, SLOT - 1) == SLOT - 1
    slot_of = jnp.bitwise_and(distance(jnp.right_shift(slot, 4)) + e, N_ENC - 1)
    source_of = jnp.bitwise_and(distance(jnp.right_shift(source, 4)) + e, N_ENC - 1)
    same = jnp.where((slot_of == source_of) & last, 1.0, 0.0).astype(BF16)
    before = jnp.where((source_of < slot_of) & last, 1.0, 0.0).astype(BF16)
    marks = ygat[t, :, 256:384]
    end_lane = lax.broadcasted_iota(jnp.int32, (SLOTS, 128), 1) == 127
    count = jnp.sum(jnp.where(end_lane, nn(same, marks), 0.0), axis=1, keepdims=True)
    start = jnp.sum(jnp.where(end_lane, nn(before, marks), 0.0), axis=1, keepdims=True)
    first = offset[0].astype(F32)
    end = jnp.max(start + count, axis=0, keepdims=True) + first
    target = lax.broadcasted_iota(jnp.int32, (SLOTS, LANES), 1).astype(F32) - first
    main, spare = slot_maps(start, count, target, 1.0)
    tmap[0] = main
    tmap[1] = spare

    eye = identity(LANES)

    def unpack(step):
        if step:
            for kind in range(CLASSES):
                part_landed(step, kind).wait_recv()
        part = tp_at(N_TP - step)
        rows = decode(ygat[part], tmap[0], tmap[1], eye).astype(BF16)
        for index in range(N_TP):
            place = lax.rem(part * N_TP + index + N_ENC - e, N_ENC)
            chunk = pl.ds(pl.multiple_of(place * CHUNK, CHUNK), CHUNK)
            turned[chunk, :] = rows[index * CHUNK : index * CHUNK + CHUNK]

    unpack(0)
    unpack(1)
    far_relay(2)
    unpack(3)
    unpack(2)
    pooled[...] = nt(eye, turned[...]).astype(BF16)

    sums[...] = jnp.zeros_like(sums)

    def forward(step, which):
        cols = pl.ds(slab_at(step, which), SLAB)
        projected = nn(pooled[0:TOKENS, :], wfull[:, cols]).astype(BF16).astype(F32)
        token = lax.broadcasted_iota(jnp.int32, projected.shape, 0).astype(F32)
        hidden = jnp.where((token >= first) & (token < end), projected, textv[:, cols].astype(F32))
        hid[:, cols] = hidden.astype(BF16)
        squares = hidden * hidden
        slopes = cotv[:, cols].astype(F32) * gain[:, cols] * hidden
        sums[0, 0:TOKENS, :] += squares[:, 0:128] + squares[:, 128:256]
        sums[1, 0:TOKENS, :] += slopes[:, 0:128] + slopes[:, 128:256]

    for copy in locals_in:
        copy.wait()
    forward(0, core)
    forward(1, core)
    forward(3, core)
    far_relay(3)
    for step in (0, 1, 3):
        from_core(step)
        forward(step, 1 - core)
    forward(2, core)
    from_core(2)
    forward(2, 1 - core)

    stats[0] = jnp.zeros((8, LANES), F32)
    stats[0, 0:1, :] = jnp.sum(jnp.transpose(sums[0]), axis=0, keepdims=True)
    stats[0, 1:2, :] = jnp.sum(jnp.transpose(sums[1]), axis=0, keepdims=True)

    def stat_copy(step):
        return pltpu.make_async_remote_copy(
            src_ref=stats.at[0], dst_ref=stats.at[step], send_sem=ss.at[step], recv_sem=sr.at[step],
            device_id={"tp": tp_at(step)}, device_id_type=MESH,
        )

    for step in (2, 1, 3):
        stat_copy(step).start()
    gh[TOKENS:LANES, :] = jnp.zeros((LANES - TOKENS, WIDE), BF16)
    for step in (2, 1, 3):
        stat_copy(step).wait_recv()
    total = (stats[0] + stats[1]) + (stats[2] + stats[3])
    inv_row = lax.rsqrt(total[0:1] / D + EPS)
    slope_row = total[1:2] / D
    inv = column(inv_row, LANES)[0:TOKENS, 0:1]
    back = column(inv_row * inv_row * inv_row * slope_row, LANES)[0:TOKENS, 0:1]

    def backward(index):
        cols = pl.ds(pl.multiple_of(index * SLAB, SLAB), SLAB)
        hidden = hid[:, cols].astype(F32)
        weighted = cotv[:, cols].astype(F32) * gain[:, cols]
        gh[0:TOKENS, cols] = (inv * weighted - back * hidden).astype(BF16)

    def normed(index):
        cols = pl.ds(pl.multiple_of(index * SLAB, SLAB), SLAB)
        mixv[:, cols] = (hid[:, cols].astype(F32) * inv * gain[:, cols]).astype(BF16)

    each(0, WIDE // SLAB, backward)

    def sum_copy(step, kind):
        rows = pl.ds(kind * GROUP, GROUP)
        return pltpu.make_async_remote_copy(
            src_ref=ysend.at[step, rows, :], dst_ref=yrecv.at[step, rows, :],
            send_sem=rs.at[part_sem(step, kind)], recv_sem=rr.at[part_sem(step, kind)],
            device_id={"tp": tp_at(step)}, device_id_type=MESH,
        )

    def back_copy(step):
        return pltpu.make_async_remote_copy(
            src_ref=bsend.at[slot_rows(place_of(step)), :], dst_ref=bret.at[slot_rows(place_of(N_ENC - step)), :],
            send_sem=gs.at[step], recv_sem=gr.at[step], device_id={"enc": enc_at(step)}, device_id_type=MESH,
        )

    def back_landed(step):
        ref = bret.at[slot_rows(place_of(N_ENC - step)), :]
        return pltpu.make_async_remote_copy(
            src_ref=ref, dst_ref=ref, send_sem=gs.at[step], recv_sem=gr.at[step],
            device_id={"enc": enc_at(step)}, device_id_type=MESH,
        )

    main, spare = tmap[0], tmap[1]

    def partial(step):
        places = [lax.rem(tp_at(step) * N_TP + index + N_ENC - e, N_ENC) for index in range(N_TP)]
        chunks = [wfull[pl.ds(pl.multiple_of(place * CHUNK, CHUNK), CHUNK), :] for place in places]
        low, high = encode(main, spare, nt(jnp.concatenate(chunks, axis=0), gh[...]).astype(BF16))
        ysend[step, :, 0:256] = low.astype(BF16)
        ysend[step, :, 256:384] = high.astype(BF16)

    for step in (2, 1, 3):
        partial(step)
        for kind in (0, 1):
            sum_copy(step, kind).start()
    partial(0)
    each(0, WIDE // SLAB, normed)
    mixed_out = pltpu.make_async_copy(mixv, mixed, ls.at[3])
    mixed_out.start()

    for kind in range(CLASSES):
        rows = slice(kind * GROUP, kind * GROUP + GROUP)
        for step in (2, 1, 3):
            sum_copy(step, kind).wait_recv()
            if kind + 2 < CLASSES:
                sum_copy(step, kind + 2).start()
        near = ysend[0, rows, :].astype(F32) + yrecv[1, rows, :].astype(F32)
        far = yrecv[2, rows, :].astype(F32) + yrecv[3, rows, :].astype(F32)
        bsend[rows, :] = (near + far).astype(BF16)
        each_of(kind, lambda step: back_copy(step).start())
    bret[0:SLOT, :] = bsend[0:SLOT, :]

    for direction in (0, 1):
        for stage in range(STAGES):
            for step in (1, 2):
                if reaches(direction, 2 * stage + step):
                    z_copy(direction, 2 * stage, step).wait_send()
            for way in (0, 1):
                x_copy(way, direction, stage).wait_send()
                x_onward(way, direction, stage).wait_send()
            for step in range(N_X):
                core_copy(step, direction, stage, core).wait_send()
    each(1, N_ENC, lambda step: pooled_copy(step).wait_send())
    for step in range(1, N_TP):
        stat_copy(step).wait_send()
        for kind in range(CLASSES):
            part_copy(step, kind).wait_send()

    for step in range(1, N_TP):
        for kind in range(CLASSES):
            sum_copy(step, kind).wait_send()
    each(1, N_ENC, lambda step: back_landed(step).wait_recv())
    grads[...] = decode(bret[...], fmap[0], fmap[1], identity(LANES)).astype(BF16)
    each(1, N_ENC, lambda step: back_copy(step).wait_send())
    mixed_out.wait()


def body(frames, proj_weight, text_emb, norm_gain, cotangent, counts, offsets):
    any_space = pl.BlockSpec(memory_space=pl.ANY)
    vmem = pl.BlockSpec(memory_space=pltpu.VMEM)
    smem = pl.BlockSpec(memory_space=pltpu.SMEM)
    dma = pltpu.SemaphoreType.DMA
    mixed, grads = pl.pallas_call(
        kernel,
        out_shape=(
            jax.ShapeDtypeStruct((TOKENS, WIDE), BF16),
            jax.ShapeDtypeStruct((PART, LANES), BF16),
        ),
        in_specs=[any_space] * 6 + [smem],
        out_specs=(any_space, vmem),
        scratch_shapes=[
            pltpu.VMEM((PART, LANES), BF16),
            pltpu.VMEM((1, WIDE), F32),
            pltpu.VMEM((1, N_ENC), jnp.int32),
            pltpu.VMEM((N_ENC * CHUNK, WIDE), BF16),
            pltpu.VMEM((TOKENS, WIDE), BF16),
            pltpu.VMEM((TOKENS, WIDE), BF16),
            pltpu.VMEM((TOKENS, WIDE), BF16),
            pltpu.VMEM((LANES, WIDE), BF16),
            pltpu.VMEM((TOKENS, WIDE), BF16),
            pltpu.VMEM((N_ENC * CHUNK, LANES), BF16),
            pltpu.VMEM((LANES, N_ENC * CHUNK), BF16),
            pltpu.VMEM((SLOTS, LANES), BF16),
            pltpu.VMEM((N_TP, SLOTS, LANES), BF16),
            pltpu.VMEM((N_TP, SLOTS, LANES), BF16),
            pltpu.VMEM((N_TP, SLOTS, LANES), BF16),
            pltpu.VMEM((N_TP, 8, LANES), F32),
            pltpu.VMEM((2, LANES, 128), F32),
            pltpu.VMEM((SLOTS, LANES), BF16),
            pltpu.VMEM((SLOTS, LANES), BF16),
            pltpu.VMEM((2, SLOTS, LANES), BF16),
            pltpu.VMEM((2, SLOTS, LANES), BF16),
            *[dma((4 * STAGES,)) for _ in range(6)],
            *[dma((8 * STAGES,)) for _ in range(2)],
            *[dma((N_ENC,)) for _ in range(2)],
            *[dma((N_TP * CLASSES,)) for _ in range(2)],
            *[dma((N_TP,)) for _ in range(2)],
            *[dma((N_TP * CLASSES,)) for _ in range(2)],
            *[dma((N_ENC,)) for _ in range(2)],
            dma((7,)),
        ],
        compiler_params=pltpu.CompilerParams(
            collective_id=0, has_side_effects=True, vmem_limit_bytes=56 * 1024 * 1024
        ),
    )(frames.T, proj_weight, text_emb, norm_gain.reshape(1, WIDE), cotangent, counts, offsets)
    return mixed, grads.T


def solution(mesh):
    in_specs = (
        P(("enc", "seq"), "tp"),
        P("enc", "tp"),
        P(("enc", "seq"), "tp"),
        P("tp"),
        P(("enc", "seq"), "tp"),
        P(("enc", "seq"), None),
        P(("enc", "seq")),
    )
    out_specs = (P(("enc", "seq"), "tp"), P(("enc", "seq"), "tp"))
    return jax.shard_map(body, mesh=mesh, in_specs=in_specs, out_specs=out_specs, check_vma=False)
```

time: 97.5 us -> 86.3 us (0.89)
  the two profiles are of different devices: /device:TPU:32 before, /device:TPU:8 now
where the time goes in v2:
time: 86.3 us; the launch traced here: 86.1 us
  Pallas kernels  81.6 us (95%)
  local copies, waits for them, and re-layouts  3.26 us (4%)
  between operations  1.3 us (2%)
    pallas_call x1, Pallas kernels, body(): pl.pallas_call(kernel, out_shape=(jax.ShapeDtypeStruct((TOKENS, WIDE), BF...  81.6 us
    unnamed x4, local copies, waits for them, and re-layouts  3.26 us

profile of v2, /device:TPU:8, one launch (start us, length us, event | category | flops | bytes accessed | tf_op | source)
XLA Modules:
  0.0 86.1 jit_solution(6077472685477801904)
XLA Ops:
  1.3 81.6 %shard_map.86 = (bf16[320,2048]{1,0:T(8,128)(2,1)}, bf16[320,384]{1,0:T(8,128)(2,1)}) custom-call(bf16[320,384]{1,0:T(8,128)(2,1)} %bitcast.3, bf16[80,2048]{1,0:T(8,128)(2,1)} %weight.1, bf16[320,2048]{1,0:T(8,128)(2,1)} %text.1, f32[1,2048]{1,0:T(1,128)} %bitcast.5, bf16[320,2048]{1,0:T(8,128)(2,1)} %cot.1, s32[1,16]{1,0:T(1,128)} %counts_in.1, ...), custom_call_target="tpu_custom_call" | custom-call | tf_op jit(solution)/shard_map/pallas_call | solution.py:515
  82.8 0.0 copy-start
  82.9 2.6 %copy.12 = bf16[320,2048]{1,0:T(8,128)(2,1)} copy(bf16[320,2048]{1,0:T(8,128)(2,1)} %get-tuple-element.8) | data formatting | bytes 2621440
  85.4 0.0 copy-done
  85.4 0.7 copy.13
Async XLA Ops:
  82.8 2.6 %copy-start = (bf16[320,384]{1,0:T(8,128)(2,1)S(1)}, bf16[320,384]{1,0:T(8,128)(2,1)}, u32[]{:S(2)}) copy-start(bf16[320,384]{1,0:T(8,128)(2,1)} %get-tuple-element.5) | copy-start | bytes 737284

commit v3 on v2

--- a/solution.py
+++ b/solution.py
@@ -307,32 +307,30 @@
         for step in (2, 1, 3):
             part_copy(step, kind).start()
 
+    pooled_sends(0)
     z_relay(0)
-    pooled_sends(0)
+    pooled_sends(3)
     seq_sends(0)
     z_relay(1)
-    pooled_sends(3)
+    pooled_sends(2)
+    pooled_sends(1)
     seq_sends(1)
     locals_in[0].start()
     locals_in[1].start()
     z_relay(2)
-    pooled_sends(2)
-    pooled_sends(1)
     seq_sends(2)
     locals_in[2].start()
     locals_in[3].start()
     x_relay(0)
     pass_on(0)
+    pass_on(1)
     z_relay(3)
     seq_sends(3)
+    pass_on(2)
     x_relay(1)
-    pass_on(1)
+    pass_on(3)
     x_relay(2)
-    pass_on(2)
     far_relay(0)
-    x_relay(3)
-    pass_on(3)
-    far_relay(1)
 
     slot = lax.broadcasted_iota(jnp.int32, (SLOTS, SLOTS), 0)
     source = lax.broadcasted_iota(jnp.int32, (SLOTS, SLOTS), 1)
@@ -352,6 +350,9 @@
     tmap[0] = main
     tmap[1] = spare
 
+    x_relay(3)
+    far_relay(1)
+
     eye = identity(LANES)
 
     def unpack(step):
@@ -388,9 +389,9 @@
     for copy in locals_in:
         copy.wait()
     forward(0, core)
+    far_relay(3)
     forward(1, core)
     forward(3, core)
-    far_relay(3)
     for step in (0, 1, 3):
         from_core(step)
         forward(step, 1 - core)
@@ -411,77 +412,6 @@
     for step in (2, 1, 3):
         stat_copy(step).start()
     gh[TOKENS:LANES, :] = jnp.zeros((LANES - TOKENS, WIDE), BF16)
-    for step in (2, 1, 3):
-        stat_copy(step).wait_recv()
-    total = (stats[0] + stats[1]) + (stats[2] + stats[3])
-    inv_row = lax.rsqrt(total[0:1] / D + EPS)
-    slope_row = total[1:2] / D
-    inv = column(inv_row, LANES)[0:TOKENS, 0:1]
-    back = column(inv_row * inv_row * inv_row * slope_row, LANES)[0:TOKENS, 0:1]
-
-    def backward(index):
-        cols = pl.ds(pl.multiple_of(index * SLAB, SLAB), SLAB)
-        hidden = hid[:, cols].astype(F32)
-        weighted = cotv[:, cols].astype(F32) * gain[:, cols]
-        gh[0:TOKENS, cols] = (inv * weighted - back * hidden).astype(BF16)
-
-    def normed(index):
-        cols = pl.ds(pl.multiple_of(index * SLAB, SLAB), SLAB)
-        mixv[:, cols] = (hid[:, cols].astype(F32) * inv * gain[:, cols]).astype(BF16)
-
-    each(0, WIDE // SLAB, backward)
-
-    def sum_copy(step, kind):
-        rows = pl.ds(kind * GROUP, GROUP)
-        return pltpu.make_async_remote_copy(
-            src_ref=ysend.at[step, rows, :], dst_ref=yrecv.at[step, rows, :],
-            send_sem=rs.at[part_sem(step, kind)], recv_sem=rr.at[part_sem(step, kind)],
-            device_id={"tp": tp_at(step)}, device_id_type=MESH,
-        )
-
-    def back_copy(step):
-        return pltpu.make_async_remote_copy(
-            src_ref=bsend.at[slot_rows(place_of(step)), :], dst_ref=bret.at[slot_rows(place_of(N_ENC - step)), :],
-            send_sem=gs.at[step], recv_sem=gr.at[step], device_id={"enc": enc_at(step)}, device_id_type=MESH,
-        )
-
-    def back_landed(step):
-        ref = bret.at[slot_rows(place_of(N_ENC - step)), :]
-        return pltpu.make_async_remote_copy(
-            src_ref=ref, dst_ref=ref, send_sem=gs.at[step], recv_sem=gr.at[step],
-            device_id={"enc": enc_at(step)}, device_id_type=MESH,
-        )
-
-    main, spare = tmap[0], tmap[1]
-
-    def partial(step):
-        places = [lax.rem(tp_at(step) * N_TP + index + N_ENC - e, N_ENC) for index in range(N_TP)]
-        chunks = [wfull[pl.ds(pl.multiple_of(place * CHUNK, CHUNK), CHUNK), :] for place in places]
-        low, high = encode(main, spare, nt(jnp.concatenate(chunks, axis=0), gh[...]).astype(BF16))
-        ysend[step, :, 0:256] = low.astype(BF16)
-        ysend[step, :, 256:384] = high.astype(BF16)
-
-    for step in (2, 1, 3):
-        partial(step)
-        for kind in (0, 1):
-            sum_copy(step, kind).start()
-    partial(0)
-    each(0, WIDE // SLAB, normed)
-    mixed_out = pltpu.make_async_copy(mixv, mixed, ls.at[3])
-    mixed_out.start()
-
-    for kind in range(CLASSES):
-        rows = slice(kind * GROUP, kind * GROUP + GROUP)
-        for step in (2, 1, 3):
-            sum_copy(step, kind).wait_recv()
-            if kind + 2 < CLASSES:
-                sum_copy(step, kind + 2).start()
-        near = ysend[0, rows, :].astype(F32) + yrecv[1, rows, :].astype(F32)
-        far = yrecv[2, rows, :].astype(F32) + yrecv[3, rows, :].astype(F32)
-        bsend[rows, :] = (near + far).astype(BF16)
-        each_of(kind, lambda step: back_copy(step).start())
-    bret[0:SLOT, :] = bsend[0:SLOT, :]
-
     for direction in (0, 1):
         for stage in range(STAGES):
             for step in (1, 2):
@@ -492,6 +422,82 @@
                 x_onward(way, direction, stage).wait_send()
             for step in range(N_X):
                 core_copy(step, direction, stage, core).wait_send()
+
+    for step in (2, 1, 3):
+        stat_copy(step).wait_recv()
+    total = (stats[0] + stats[1]) + (stats[2] + stats[3])
+    inv_row = lax.rsqrt(total[0:1] / D + EPS)
+    slope_row = total[1:2] / D
+    inv = column(inv_row, LANES)[0:TOKENS]
+    back = column(inv_row * inv_row * inv_row * slope_row, LANES)[0:TOKENS]
+    inv = jnp.concatenate([inv, inv], axis=1)
+    back = jnp.concatenate([back, back], axis=1)
+
+    def backward(index):
+        cols = pl.ds(pl.multiple_of(index * SLAB, SLAB), SLAB)
+        hidden = hid[:, cols].astype(F32)
+        weighted = cotv[:, cols].astype(F32) * gain[:, cols]
+        gh[0:TOKENS, cols] = (inv * weighted - back * hidden).astype(BF16)
+
+    def normed(index):
+        cols = pl.ds(pl.multiple_of(index * SLAB, SLAB), SLAB)
+        mixv[:, cols] = (hid[:, cols].astype(F32) * inv * gain[:, cols]).astype(BF16)
+
+    each(0, WIDE // SLAB, backward)
+
+    def sum_copy(step, kind):
+        rows = pl.ds(kind * GROUP, GROUP)
+        return pltpu.make_async_remote_copy(
+            src_ref=ysend.at[step, rows, :], dst_ref=yrecv.at[step, rows, :],
+            send_sem=rs.at[part_sem(step, kind)], recv_sem=rr.at[part_sem(step, kind)],
+            device_id={"tp": tp_at(step)}, device_id_type=MESH,
+        )
+
+    def back_copy(step):
+        return pltpu.make_async_remote_copy(
+            src_ref=bsend.at[slot_rows(place_of(step)), :], dst_ref=bret.at[slot_rows(place_of(N_ENC - step)), :],
+            send_sem=gs.at[step], recv_sem=gr.at[step], device_id={"enc": enc_at(step)}, device_id_type=MESH,
+        )
+
+    def back_landed(step):
+        ref = bret.at[slot_rows(place_of(N_ENC - step)), :]
+        return pltpu.make_async_remote_copy(
+            src_ref=ref, dst_ref=ref, send_sem=gs.at[step], recv_sem=gr.at[step],
+            device_id={"enc": enc_at(step)}, device_id_type=MESH,
+        )
+
+    main, spare = tmap[0], tmap[1]
+
+    def partial(step):
+        places = [lax.rem(tp_at(step) * N_TP + index + N_ENC - e, N_ENC) for index in range(N_TP)]
+        chunks = [wfull[pl.ds(pl.multiple_of(place * CHUNK, CHUNK), CHUNK), :] for place in places]
+        low, high = encode(main, spare, nt(jnp.concatenate(chunks, axis=0), gh[...]).astype(BF16))
+        ysend[step, :, 0:256] = low.astype(BF16)
+        ysend[step, :, 256:384] = high.astype(BF16)
+
+    for step in (2, 1, 3):
+        partial(step)
+        for kind in (0, 1):
+            sum_copy(step, kind).start()
+    partial(0)
+    for step in (2, 1, 3):
+        sum_copy(step, 2).start()
+    each(0, WIDE // SLAB, normed)
+    for step in (2, 1, 3):
+        sum_copy(step, 3).start()
+    mixed_out = pltpu.make_async_copy(mixv, mixed, ls.at[3])
+    mixed_out.start()
+
+    for kind in range(CLASSES):
+        rows = slice(kind * GROUP, kind * GROUP + GROUP)
+        for step in (2, 1, 3):
+            sum_copy(step, kind).wait_recv()
+        near = ysend[0, rows, :].astype(F32) + yrecv[1, rows, :].astype(F32)
+        far = yrecv[2, rows, :].astype(F32) + yrecv[3, rows, :].astype(F32)
+        bsend[rows, :] = (near + far).astype(BF16)
+        each_of(kind, lambda step: back_copy(step).start())
+    bret[0:SLOT, :] = bsend[0:SLOT, :]
+
     each(1, N_ENC, lambda step: pooled_copy(step).wait_send())
     for step in range(1, N_TP):
         stat_copy(step).wait_send()

time: 86.3 us -> 84.7 us (0.981)
  the two profiles are of different devices: /device:TPU:8 before, /device:TPU:32 now
where the time goes in v3:
time: 84.7 us; the launch traced here: 84.5 us
  Pallas kernels  80 us (94%)
  local copies, waits for them, and re-layouts  3.26 us (4%)
  between operations  1.3 us (2%)
    pallas_call x1, Pallas kernels, body(): pl.pallas_call(kernel, out_shape=(jax.ShapeDtypeStruct((TOKENS, WIDE), BF...  80 us
    unnamed x4, local copies, waits for them, and re-layouts  3.26 us

profile of v3, /device:TPU:32, one launch (start us, length us, event | category | flops | bytes accessed | tf_op | source)
XLA Modules:
  0.0 84.5 jit_solution(17175259920610544370)
XLA Ops:
  1.3 80.0 %shard_map.86 = (bf16[320,2048]{1,0:T(8,128)(2,1)}, bf16[320,384]{1,0:T(8,128)(2,1)}) custom-call(bf16[320,384]{1,0:T(8,128)(2,1)} %bitcast.3, bf16[80,2048]{1,0:T(8,128)(2,1)} %weight.1, bf16[320,2048]{1,0:T(8,128)(2,1)} %text.1, f32[1,2048]{1,0:T(1,128)} %bitcast.5, bf16[320,2048]{1,0:T(8,128)(2,1)} %cot.1, s32[1,16]{1,0:T(1,128)} %counts_in.1, ...), custom_call_target="tpu_custom_call" | custom-call | tf_op jit(solution)/shard_map/pallas_call | solution.py:521
  81.3 0.0 copy-start
  81.3 2.6 %copy.12 = bf16[320,2048]{1,0:T(8,128)(2,1)} copy(bf16[320,2048]{1,0:T(8,128)(2,1)} %get-tuple-element.8) | data formatting | bytes 2621440
  83.8 0.0 copy-done
  83.8 0.7 copy.13
Async XLA Ops:
  81.3 2.6 %copy-start = (bf16[320,384]{1,0:T(8,128)(2,1)S(1)}, bf16[320,384]{1,0:T(8,128)(2,1)}, u32[]{:S(2)}) copy-start(bf16[320,384]{1,0:T(8,128)(2,1)} %get-tuple-element.5) | copy-start | bytes 737284

commit v4 on v3

--- a/solution.py
+++ b/solution.py
@@ -326,10 +326,10 @@
     pass_on(1)
     z_relay(3)
     seq_sends(3)
+    x_relay(1)
     pass_on(2)
-    x_relay(1)
+    x_relay(2)
     pass_on(3)
-    x_relay(2)
     far_relay(0)
 
     slot = lax.broadcasted_iota(jnp.int32, (SLOTS, SLOTS), 0)
@@ -479,9 +479,9 @@
         partial(step)
         for kind in (0, 1):
             sum_copy(step, kind).start()
-    partial(0)
     for step in (2, 1, 3):
         sum_copy(step, 2).start()
+    partial(0)
     each(0, WIDE // SLAB, normed)
     for step in (2, 1, 3):
         sum_copy(step, 3).start()

time: 84.7 us -> 84.6 us (level)
  no operation moved by 1% of the time
where the time goes in v4:
time: 84.6 us; the launch traced here: 84.5 us
  Pallas kernels  79.9 us (94%)
  local copies, waits for them, and re-layouts  3.26 us (4%)
  between operations  1.3 us (2%)
    pallas_call x1, Pallas kernels, body(): pl.pallas_call(kernel, out_shape=(jax.ShapeDtypeStruct((TOKENS, WIDE), BF...  79.9 us
    unnamed x4, local copies, waits for them, and re-layouts  3.26 us

profile of v4, /device:TPU:32, one launch (start us, length us, event | category | flops | bytes accessed | tf_op | source)
XLA Modules:
  0.0 84.5 jit_solution(5713321452087963972)
XLA Ops:
  1.3 79.9 %shard_map.86 = (bf16[320,2048]{1,0:T(8,128)(2,1)}, bf16[320,384]{1,0:T(8,128)(2,1)}) custom-call(bf16[320,384]{1,0:T(8,128)(2,1)} %bitcast.3, bf16[80,2048]{1,0:T(8,128)(2,1)} %weight.1, bf16[320,2048]{1,0:T(8,128)(2,1)} %text.1, f32[1,2048]{1,0:T(1,128)} %bitcast.5, bf16[320,2048]{1,0:T(8,128)(2,1)} %cot.1, s32[1,16]{1,0:T(1,128)} %counts_in.1, ...), custom_call_target="tpu_custom_call" | custom-call | tf_op jit(solution)/shard_map/pallas_call | solution.py:521
  81.2 0.0 copy-start
  81.2 2.6 %copy.12 = bf16[320,2048]{1,0:T(8,128)(2,1)} copy(bf16[320,2048]{1,0:T(8,128)(2,1)} %get-tuple-element.8) | data formatting | bytes 2621440
  83.8 0.0 copy-done
  83.8 0.7 copy.13
Async XLA Ops:
  81.2 2.6 %copy-start = (bf16[320,384]{1,0:T(8,128)(2,1)S(1)}, bf16[320,384]{1,0:T(8,128)(2,1)}, u32[]{:S(2)}) copy-start(bf16[320,384]{1,0:T(8,128)(2,1)} %get-tuple-element.5) | copy-start | bytes 737284
